TPU v7x, 256 devices: a whole 4x4x8 slice. The times are simulated.
256 devices in a mesh: row: 8 (over z_lo, x), col: 32 (over y, z_hi, core).
Axes of the slice: x: 4, y: 4, z: 8 (z_hi: 4, z_lo: 2; z = z_hi * 2 + z_lo), core: 2. Of those that a mesh axis runs over, the one named last changes fastest.
Arguments:
- tokens: bfloat16 [512, 8192], P('col', 'row'), may hold values from -6 to 6
- grad_output: bfloat16 [512, 8192], P('col', 'row'), may hold values from -1.5 to 1.5
- gate_weight: bfloat16 [8192, 28672], P('row', 'col'), may hold values from -0.0625 to 0.0625
- up_weight: bfloat16 [8192, 28672], P('row', 'col'), may hold values from -0.0625 to 0.0625
- down_weight: bfloat16 [28672, 8192], P('col', 'row'), may hold values from -0.03125 to 0.03125
- segment_ids: int32 [512], replicated, may hold values from 0 to 63, never falling along the last dimension, each value on 1 to 16 neighbouring positions
Outputs:
- grad_tokens: bfloat16 [512, 8192], P('col', 'row')
- grad_gate: bfloat16 [8192, 28672], P('row', 'col')
- grad_up: bfloat16 [8192, 28672], P('row', 'col')
- grad_down: bfloat16 [28672, 8192], P('col', 'row')
Inputs may be any that keep to these rules, and one draw needn't show every extreme that they name: `segment_ids`: segment ids never fall along the tokens; each of the 64 passages holds 1 to 16 tokens, one exactly 16.
All inputs are finite; a program needn't handle non-finite values.
Results may differ from a plain program's by a relative error of at most 0.033.
Values may be sent and summed in bfloat16 or wider, within the bound.
A program may use at most 64 MiB of HBM per device.

v0:
```python
import jax
import jax.numpy as jnp
from jax import lax
from jax.sharding import PartitionSpec as P

TOKENS = 512
SEGS = 64


def elementwise(gate, up, d_hidden):
    sig = jax.nn.sigmoid(gate)
    hidden = (gate * sig * up).astype(jnp.bfloat16)
    d_gate = (d_hidden * up * sig * (1.0 + gate * (1.0 - sig))).astype(jnp.bfloat16)
    d_up = (d_hidden * gate * sig).astype(jnp.bfloat16)
    return (hidden, d_gate, d_up)


def per_device(tokens, grad_output, gate_weight, up_weight, down_weight, segment_ids):
    token_all, grad_all = (
        lax.all_gather(tokens, "col", axis=0, tiled=True),
        lax.all_gather(grad_output, "col", axis=0, tiled=True),
    )
    same = segment_ids[:, None] == segment_ids[None, :]
    counts = jnp.sum(same.astype(jnp.float32), axis=1)
    token_weight = TOKENS / SEGS / counts
    weighted = (grad_all.astype(jnp.float32) * token_weight[:, None]).astype(jnp.bfloat16)
    gate_part = jnp.dot(token_all, gate_weight, preferred_element_type=jnp.float32)
    up_part = jnp.dot(token_all, up_weight, preferred_element_type=jnp.float32)
    back_part = jnp.einsum("td,fd->tf", weighted, down_weight, preferred_element_type=jnp.float32)
    gate, up, d_hidden = (
        lax.psum(gate_part.astype(jnp.bfloat16), "row").astype(jnp.float32),
        lax.psum(up_part.astype(jnp.bfloat16), "row").astype(jnp.float32),
        lax.psum(back_part.astype(jnp.bfloat16), "row").astype(jnp.float32),
    )
    hidden, d_gate, d_up = elementwise(gate, up, d_hidden)
    grad_down = jnp.einsum(
        "tf,td->fd", hidden, weighted, preferred_element_type=jnp.float32
    ).astype(jnp.bfloat16)
    grad_gate = jnp.einsum(
        "td,tf->df", token_all, d_gate, preferred_element_type=jnp.float32
    ).astype(jnp.bfloat16)
    grad_up = jnp.einsum("td,tf->df", token_all, d_up, preferred_element_type=jnp.float32).astype(
        jnp.bfloat16
    )
    first = jnp.einsum("tf,df->td", d_gate, gate_weight, preferred_element_type=jnp.float32)
    second = jnp.einsum("tf,df->td", d_up, up_weight, preferred_element_type=jnp.float32)
    grad_rows = lax.psum_scatter(
        (first + second).astype(jnp.bfloat16), "col", scatter_dimension=0, tiled=True
    )
    return (grad_rows, grad_gate, grad_up, grad_down)


def solution(mesh):
    in_specs = (
        P("col", "row"),
        P("col", "row"),
        P("row", "col"),
        P("row", "col"),
        P("col", "row"),
        P(),
    )
    out_specs = (P("col", "row"), P("row", "col"), P("row", "col"), P("col", "row"))
    return jax.shard_map(
        per_device, mesh=mesh, in_specs=in_specs, out_specs=out_specs, check_vma=False
    )
```

profile of v0, /device:TPU:2, one launch (start us, length us, event | category | flops | bytes accessed | tf_op | source)
XLA Modules:
  0.0 315.2 jit_solution(2727287761574044139)
XLA Ops:
  7.2 0.0 copy-start
  7.2 0.0 all-gather.5.cloned.1.call-start
  7.2 0.7 all-gather.5.cloned.1.call-update
  7.9 0.0 all-gather.3.cloned.1.call-start
  8.0 0.7 all-gather.3.cloned.1.call-update
  8.7 0.0 all-reduce.3.cloned.1.call-start
  8.7 1.0 convert_reduce_fusion
  9.7 55.9 %all-gather.5.cloned.1.call-done = bf16[512,1024]{1,0:T(8,128)(2,1)} async-done(((bf16[16,1024]{1,0:T(8,128)(2,1)}), bf16[512,1024]{1,0:T(8,128)(2,1)}) %all-gather.5.cloned.1.call-update) | async-done | bytes 1048592 | tf_op jit(solution)/shard_map/all_gather | solution.py:20
  65.6 0.0 copy-start.6
  65.6 4.1 %convolution_convert_fusion.2 = bf16[512,896]{1,0:T(8,128)(2,1)} fusion(bf16[512,1024]{1,0:T(8,128)(2,1)} %all-gather.5.cloned.1.call-done, bf16[1024,896]{1,0:T(8,128)(2,1)} %param.9), kind=kOutput, calls=%fused_computation.22 | convolution fusion | flops 939982848 | bytes 3801088 | tf_op jit(solution)/shard_map/dot_general | solution.py:28
  69.7 0.0 copy-done
  69.7 0.0 copy-done.6
  69.7 2.2 convolution_convert_fusion.1
  71.9 45.8 %all-gather.3.cloned.1.call-done = bf16[512,1024]{1,0:T(8,128)(2,1)} async-done(((bf16[16,1024]{1,0:T(8,128)(2,1)}), bf16[512,1024]{1,0:T(8,128)(2,1)}) %all-gather.3.cloned.1.call-update) | async-done | bytes 1048592 | tf_op jit(solution)/shard_map/all_gather | solution.py:21
  117.7 4.0 %convolution_convert_fusion.3 = bf16[512,896]{1,0:T(8,128)(2,1)} fusion(bf16[896,1024]{1,0:T(8,128)(2,1)} %param.10, bf16[512,1024]{1,0:T(8,128)(2,1)} %all-gather.3.cloned.1.call-done, f32[512]{0:T(512)S(1)} %broadcast_divide_fusion), kind=kOutput, calls=%fused_computation.23 | convolution fusion | flops 941555712 | bytes 3803136 | tf_op jit(solution)/shard_map/td,fd->tf/dot_general | solution.py:29
  121.7 0.0 all-reduce.3.cloned.1.call-update
  121.8 0.0 reduce-scatter.2.cloned.1.call-start
  121.8 88.5 %all-reduce.3.cloned.1.call-done = (bf16[512,896]{1,0:T(8,128)(2,1)}, bf16[512,896]{1,0:T(8,128)(2,1)}, bf16[512,896]{1,0:T(8,128)(2,1)}) async-done(((bf16[512,896]{1,0:T(8,128)(2,1)}, bf16[512,896]{1,0:T(8,128)(2,1)}, bf16[512,896]{1,0:T(8,128)(2,1)}), (bf16[512,896]{1,0:T(8,128)(2,1)}, bf16[512,896]{1,0:T(8,128)(2,1)}, bf16[512,896]{1,0:T(8,128)(2,1)})) %all-reduce.3.cloned.1.call-update) | async-done | bytes 2752528 | tf_op jit(solution)/shard_map/psum | solution.py:32
  210.3 2.6 fusion.2
  212.9 0.0 copy-start.4
  212.9 0.9 copy-done.4
  213.8 0.0 copy-start.2
  213.8 0.0 copy-start.3
  213.8 0.0 copy-start.5
  213.8 1.3 fusion.15
  215.1 0.0 copy-done.2
  215.1 0.2 copy-done.3
  215.3 0.6 copy-done.5
  215.9 2.3 add_convert_fusion
  218.2 0.0 reduce-scatter.2.cloned.1.call-update
  218.2 3.9 %convert_bitcast_fusion.1 = bf16[1024,896]{0,1:T(8,128)(2,1)} fusion(bf16[512,896]{1,0:T(8,128)(2,1)} %copy-done.4, bf16[512,1024]{1,0:T(8,128)(2,1)} %all-gather.5.cloned.1.call-done), kind=kOutput, calls=%fused_computation.19 | convolution fusion | flops 940441600 | bytes 3801088 | tf_op jit(solution)/shard_map/td,tf->df/dot_general | solution.py:39
  222.1 3.8 %copy.12 = bf16[1024,896]{1,0:T(8,128)(2,1)} copy(bf16[1024,896]{0,1:T(8,128)(2,1)} %convert_bitcast_fusion.1) | data formatting | bytes 3670016
  225.9 4.0 %convert_bitcast_fusion = bf16[1024,896]{0,1:T(8,128)(2,1)} fusion(bf16[512,1024]{1,0:T(8,128)(2,1)} %all-gather.5.cloned.1.call-done, bf16[512,896]{1,0:T(8,128)(2,1)S(1)} %copy-done.2, bf16[512,896]{1,0:T(8,128)(2,1)} %get-tuple-element.13), kind=kOutput, calls=%fused_computation.18 | convolution fusion | flops 944111616 | bytes 4718592 | tf_op jit(solution)/shard_map/td,tf->df/dot_general | solution.py:42
  229.9 0.0 copy-start.1
  229.9 3.9 %copy.13 = bf16[1024,896]{1,0:T(8,128)(2,1)} copy(bf16[1024,896]{0,1:T(8,128)(2,1)} %convert_bitcast_fusion) | data formatting | bytes 3670016
  233.8 0.0 copy-done.1
  233.8 4.2 %convolution_convert_fusion = bf16[896,1024]{1,0:T(8,128)(2,1)} fusion(bf16[512,896]{1,0:T(8,128)(2,1)S(1)} %copy-done.1, bf16[512,896]{1,0:T(8,128)(2,1)} %get-tuple-element.14, bf16[512,1024]{1,0:T(8,128)(2,1)} %all-gather.3.cloned.1.call-done, f32[512]{0:T(512)S(1)} %broadcast_divide_fusion), kind=kOutput, calls=%fused_computation.20 | convolution fusion | flops 945684480 | bytes 4720640 | tf_op jit(solution)/shard_map/tf,td->fd/dot_general | solution.py:36
  238.0 70.7 %reduce-scatter.2.cloned.1.call-done = bf16[16,1024]{1,0:T(8,128)(2,1)} async-done(((bf16[512,1024]{1,0:T(8,128)(2,1)}), bf16[16,1024]{1,0:T(8,128)(2,1)}) %reduce-scatter.2.cloned.1.call-update) | async-done | bytes 32784 | tf_op jit(solution)/shard_map/reduce_scatter | solution.py:47
  (1 shorter events, 0.0 us)
Async XLA Ops:
  7.2 62.5 %copy-start = (bf16[1024,896]{1,0:T(8,128)(2,1)S(1)}, bf16[1024,896]{1,0:T(8,128)(2,1)}, u32[]{:S(2)}) copy-start(bf16[1024,896]{1,0:T(8,128)(2,1)} %param.8) | copy-start | bytes 5505028
  7.2 58.4 %all-gather.5.cloned.1.call-start = ((), (), s32[]{:S(2)}) async-start(), calls=%async_computation.2 | async-start | bytes 1081344 | tf_op jit(solution)/shard_map/all_gather | solution.py:20
  7.9 109.8 %all-gather.3.cloned.1.call-start = ((), (), s32[]{:S(2)}) async-start(), calls=%async_computation.1 | async-start | bytes 1081344 | tf_op jit(solution)/shard_map/all_gather | solution.py:21
  8.7 201.7 %all-reduce.3.cloned.1.call-start = ((), (), s32[]{:S(2)}) async-start(), calls=%async_computation.4 | async-start | bytes 5505024 | tf_op jit(solution)/shard_map/psum | solution.py:32
  65.6 4.1 %copy-start.6 = (bf16[512,1024]{1,0:T(8,128)(2,1)S(1)}, bf16[512,1024]{1,0:T(8,128)(2,1)}, u32[]{:S(2)}) copy-start(bf16[512,1024]{1,0:T(8,128)(2,1)} %all-gather.5.cloned.1.call-done) | copy-start | bytes 3145732
  121.8 186.9 %reduce-scatter.2.cloned.1.call-start = ((), (), s32[]{:S(2)}) async-start(), calls=%async_computation.3 | async-start | bytes 1081344 | tf_op jit(solution)/shard_map/reduce_scatter | solution.py:47
  212.9 0.9 copy-start.4
  213.8 1.3 copy-start.2
  213.8 1.5 copy-start.3
  213.8 2.1 copy-start.5
  229.9 3.9 %copy-start.1 = (bf16[512,896]{1,0:T(8,128)(2,1)S(1)}, bf16[512,896]{1,0:T(8,128)(2,1)}, u32[]{:S(2)}) copy-start(bf16[512,896]{1,0:T(8,128)(2,1)} %get-tuple-element.12) | copy-start | bytes 2752516
Sparse Core Ops, SparseCore 0:
  10.6 54.9 all-gather.4
  68.2 49.4 all-gather.2
  121.9 88.3 all-reduce.2
  218.4 90.3 reduce-scatter.1
where the time goes:
time: 316 us; the launch traced here: 315 us
  waiting for transfers between devices  262 us (83%)
  matrix products  26 us (8%)
  between operations  13.8 us (4%)
  local copies, waits for them, and re-layouts  9.39 us (3%)
  other arithmetic  3.57 us (1%)
    psum x1, waiting for transfers between devices, per_device(): lax.psum(up_part.astype(jnp.bfloat16), 'row').astype(jnp.float32)  88.5 us
    reduce_scatter x1, waiting for transfers between devices, per_device(): lax.psum_scatter((first + second).astype(jnp.bfloat16), 'col', scatter_di...  70.7 us
    all_gather x1, waiting for transfers between devices, per_device(): lax.all_gather(tokens, 'col', axis=0, tiled=True)  55.9 us
    all_gather x1, waiting for transfers between devices, per_device(): lax.all_gather(grad_output, 'col', axis=0, tiled=True)  45.8 us
    unnamed x16, local copies, waits for them, and re-layouts  9.39 us
  transfers between devices with their start and end apart: 4, of which 4 were waited for; matrix products, arithmetic and copies ran while one was open for 9% of the time, Pallas kernels for 0%

commit v1 on v0

v1 whole, which is shorter than its diff:
```python
import functools

import jax
import jax.numpy as jnp
from jax import lax
from jax.experimental import pallas as pl
from jax.experimental.pallas import tpu as pltpu
from jax.sharding import PartitionSpec as P

MESH = pl.DeviceIdType.MESH
BF = jnp.bfloat16
F32 = jnp.float32
TOKENS = 512
SEGS = 64
G = 16
ORDER = (0, 1, 3, 2)
KINDS = "xxxx"


def nn(a, b):
    return jnp.dot(a, b, preferred_element_type=F32)


def nt(a, b):
    return lax.dot_general(a, b, (((1,), (1,)), ((), ())), preferred_element_type=F32)


def kernel(
    tokens, grad, ids, gate_w, up_w, down_w,
    o_tok, o_gate, o_up, o_down,
    tw, gst, gw, uw, dw, part, relp, relm, land, zs, zr, zbig, hid, gt, sib, ysend, yland,
    zsend, zland, own, tok_t, hid_t, w_st, og, ou, od,
    ssem, loc, a_recv, p_recv, l_recv, z_recv, h_recv, h2_recv, s_recv, y_recv, zh_recv,
):
    f = gw.shape[1]
    d = gw.shape[0]
    cut = (3 * f // 256 + 1) * 128
    r, c = lax.axis_index("row"), lax.axis_index("col")
    x, zl = r % 4, r // 4
    core, zh, y = c % 2, (c // 2) % 4, c // 8
    xp, xm, x2 = (x + 1) % 4, (x + 3) % 4, (x + 2) % 4

    def at(x=x, zl=zl, y=y, zh=zh, core=core):
        return {"row": zl * 4 + x, "col": (y * 4 + zh) * 2 + core}

    dev_xp, dev_xm, dev_z, dev_core = at(x=xp), at(x=xm), at(zl=1 - zl), at(core=1 - core)
    dev_zh = [at(zh=(zh + k) % 4) for k in (1, 2, 3)]
    dev_y = [at(y=(y + k) % 4) for k in (1, 2, 3)]
    partners = [dev_xp, dev_xm, dev_z, dev_core] + dev_zh + dev_y

    barrier = pltpu.get_barrier_semaphore()
    for p in partners:
        pl.semaphore_signal(barrier, inc=1, device_id=p, device_id_type=MESH)

    first = [
        pltpu.make_async_copy(tokens, tw.at[y, core, zh, 0], loc.at[0]),
        pltpu.make_async_copy(grad, gst, loc.at[1]),
    ]
    weights = [
        pltpu.make_async_copy(gate_w, gw, loc.at[2]),
        pltpu.make_async_copy(up_w, uw, loc.at[3]),
        pltpu.make_async_copy(down_w, dw, loc.at[4]),
    ]
    for cp in first + weights:
        cp.start()

    idr = jnp.broadcast_to(ids[...].astype(F32), (G, TOKENS))
    lane = lax.broadcasted_iota(jnp.int32, (G, TOKENS), 1)
    row = lax.broadcasted_iota(jnp.int32, (G, TOKENS), 0)
    mine = jnp.sum(jnp.where(lane == c * G + row, idr, 0.0), axis=1, keepdims=True)
    count = jnp.sum(jnp.where(idr == mine, 1.0, 0.0), axis=1, keepdims=True)
    weight = (TOKENS / SEGS) / count
    for cp in first:
        cp.wait()
    tw[y, core, zh, 1] = (gst[...].astype(F32) * weight).astype(BF)
    pl.semaphore_wait(barrier, len(partners))

    sent = []

    def push(src, dst, recv, dev):
        cp = pltpu.make_async_remote_copy(
            src_ref=src, dst_ref=dst, send_sem=ssem.at[len(sent)], recv_sem=recv,
            device_id=dev, device_id_type=MESH,
        )
        cp.start()
        sent.append(cp)

    def arrived(ref, recv):
        pltpu.make_async_remote_copy(
            src_ref=ref, dst_ref=ref, send_sem=ssem.at[0], recv_sem=recv,
            device_id=dev_core, device_id_type=MESH,
        ).wait_recv()

    def spread(hh, targets):
        piece = tw.at[y, core, hh]
        for dev in targets:
            push(piece, piece, a_recv.at[y, core, hh], dev)

    def gather_own():
        spread(zh, [dev_zh[0], dev_zh[2], dev_zh[1]])
        spread(zh, [dev_y[0], dev_y[2], dev_y[1], dev_core])
        for k in (1, 3, 2):
            hh = (zh + k) % 4
            arrived(tw.at[y, core, hh], a_recv.at[y, core, hh])
            spread(hh, [dev_y[0], dev_y[2], dev_y[1], dev_core])

    def gather_far(j):
        yy = (y + ORDER[j]) % 4
        for hh in range(4):
            piece = tw.at[yy, core, hh]
            arrived(piece, a_recv.at[yy, core, hh])
            push(piece, piece, a_recv.at[yy, core, hh], dev_core)

    def multiply(j):
        yy = (y + ORDER[j]) % 4
        for hh in range(4):
            arrived(tw.at[yy, 1 - core, hh], a_recv.at[yy, 1 - core, hh])
        t = tw[yy, :, :, 0].reshape(8 * G, d)
        w = tw[yy, :, :, 1].reshape(8 * G, d)
        if j == 0:
            for cp in weights:
                cp.wait()
        part[j, :, :, :, 0:f] = nn(t, gw[...]).astype(BF).reshape(2, 4, G, f)
        part[j, :, :, :, f : 2 * f] = nn(t, uw[...]).astype(BF).reshape(2, 4, G, f)
        part[j, :, :, :, 2 * f : 3 * f] = nt(w, dw[...]).astype(BF).reshape(2, 4, G, f)
        if KINDS[j] == "z":
            push(part.at[j, 1 - zl], zbig.at[j], z_recv.at[j], dev_z)
        else:
            relay(j)
        tok_t[:, j * 8 * G : (j + 1) * 8 * G] = t.T
        w_st[j * 8 * G : (j + 1) * 8 * G, :] = w

    def span(j):
        return pl.ds(zl, 1) if KINDS[j] == "z" else pl.ds(0, 2)

    def slot(j):
        return pl.ds(0, 1) if KINDS[j] == "z" else pl.ds(0, 2)

    def relay(j):
        push(part.at[j, span(j), x2, :, :cut], relp.at[j, slot(j)], p_recv.at[j, 0], dev_xp)
        push(part.at[j, span(j), x2, :, cut:], relm.at[j, slot(j)], p_recv.at[j, 1], dev_xm)

    def pair_first(j):
        if KINDS[j] != "z":
            return
        arrived(zbig.at[j], z_recv.at[j])
        part[j, zl] = (part[j, zl].astype(F32) + zbig[j].astype(F32)).astype(BF)
        relay(j)

    def forward(j):
        s, k = span(j), slot(j)
        arrived(relp.at[j, k], p_recv.at[j, 0])
        part[j, s, xp, :, :cut] = (
            part[j, s, xp, :, :cut].astype(F32) + relp[j, k].astype(F32)
        ).astype(BF)
        push(part.at[j, s, xp], land.at[j, 0, k], l_recv.at[j, 0], dev_xp)
        arrived(relm.at[j, k], p_recv.at[j, 1])
        part[j, s, xm, :, cut:] = (
            part[j, s, xm, :, cut:].astype(F32) + relm[j, k].astype(F32)
        ).astype(BF)
        push(part.at[j, s, xm], land.at[j, 1, k], l_recv.at[j, 1], dev_xm)

    def line_sum(j, z, k):
        return part[j, z, x].astype(F32) + land[j, 0, k].astype(F32) + land[j, 1, k].astype(F32)

    def pair_last(j):
        k = slot(j)
        arrived(land.at[j, 0, k], l_recv.at[j, 0])
        arrived(land.at[j, 1, k], l_recv.at[j, 1])
        if KINDS[j] == "z":
            return
        zs[j] = line_sum(j, 1 - zl, 1 - zl).astype(BF)
        push(zs.at[j], zr.at[j], z_recv.at[j], dev_z)

    def share(j, z, xx, targets):
        piece = hid.at[j, z, xx]
        for dev in targets:
            push(piece, piece, h_recv.at[j, z, xx], dev)

    def element(j):
        if KINDS[j] == "z":
            total = line_sum(j, zl, 0)
        else:
            arrived(zr.at[j], z_recv.at[j])
            total = line_sum(j, zl, zl) + zr[j].astype(F32)
        gate, up, dh = total[:, :f], total[:, f : 2 * f], total[:, 2 * f :]
        sig = jax.nn.sigmoid(gate)
        act = gate * sig
        hid[j, zl, x, :, 0:f] = (act * up).astype(BF)
        hid[j, zl, x, :, f : 2 * f] = (dh * up * sig * (1.0 + gate * (1.0 - sig))).astype(BF)
        hid[j, zl, x, :, 2 * f : 3 * f] = (dh * act).astype(BF)
        share(j, zl, x, [dev_xp, dev_xm, dev_z])

    def pair_share(j):
        if KINDS[j] == "z":
            return
        arrived(hid.at[j, 1 - zl, x], h_recv.at[j, 1 - zl, x])
        share(j, 1 - zl, x, [dev_xp, dev_xm])

    def line_share(j):
        s = span(j)
        rows = [zl] if KINDS[j] == "z" else [0, 1]
        for src, half, dev, n in ((xm, pl.ds(0, cut), dev_xp, 0), (xp, pl.ds(cut, 3 * f - cut), dev_xm, 1)):
            for z in rows:
                arrived(hid.at[j, z, src], h_recv.at[j, z, src])
            piece = hid.at[j, s, src, :, half]
            push(piece, piece, h2_recv.at[j, n], dev)
            if KINDS[j] == "z":
                share(j, zl, src, [dev_z])

    def far_share(j):
        arrived(hid.at[j, span(j), x2, :, :cut], h2_recv.at[j, 0])
        arrived(hid.at[j, span(j), x2, :, cut:], h2_recv.at[j, 1])
        if KINDS[j] == "z":
            share(j, zl, x2, [dev_z])

    def back(j):
        if KINDS[j] == "z":
            for xx in range(4):
                arrived(hid.at[j, 1 - zl, xx], h_recv.at[j, 1 - zl, xx])
        dg = hid[j, :, :, :, f : 2 * f].reshape(8 * G, f)
        du = hid[j, :, :, :, 2 * f : 3 * f].reshape(8 * G, f)
        gt[j] = (nt(dg, gw[...]) + nt(du, uw[...])).astype(BF).reshape(2, 4, G, d)
        push(gt.at[j, 1 - core], sib.at[j], s_recv.at[j], dev_core)
        hid_t[:, j * 8 * G : (j + 1) * 8 * G] = hid[j, :, :, :, 0:f].reshape(8 * G, f).T

    def core_sum(j):
        arrived(sib.at[j], s_recv.at[j])
        if j > 0:
            ysend[j - 1] = (gt[j, core].astype(F32) + sib[j].astype(F32)).astype(BF)
            push(ysend.at[j - 1], yland.at[j - 1], y_recv.at[j - 1], dev_y[ORDER[j] - 1])

    def y_sum():
        total = gt[0, core].astype(F32) + sib[0].astype(F32)
        for k in range(3):
            arrived(yland.at[k], y_recv.at[k])
            total = total + yland[k].astype(F32)
        zsend[...] = total.astype(BF)
        for k in (1, 0, 2):
            push(zsend.at[(zh + k + 1) % 4], zland.at[k], zh_recv.at[k], dev_zh[k])

    def z_sum():
        total = zsend[zh].astype(F32)
        for k in range(3):
            arrived(zland.at[k], zh_recv.at[k])
            total = total + zland[k].astype(F32)
        o_tok[...] = total.astype(BF)

    outs = []

    def weight_grad(lhs, rhs, stage, out, sem):
        rows = 256 if lhs.shape[0] % 256 == 0 else 128
        for m in range(0, lhs.shape[0], rows):
            stage[m : m + rows, :] = nn(lhs[m : m + rows, :], rhs).astype(BF)
        cp = pltpu.make_async_copy(stage, out, loc.at[sem])
        cp.start()
        outs.append(cp)

    def grad_down():
        weight_grad(hid_t, w_st[...], od, o_down, 5)

    def grad_gate():
        weight_grad(tok_t, hid[:, :, :, :, f : 2 * f].reshape(TOKENS, f), og, o_gate, 6)

    def grad_up():
        weight_grad(tok_t, hid[:, :, :, :, 2 * f : 3 * f].reshape(TOKENS, f), ou, o_up, 7)

    gather_own()
    multiply(0)
    gather_far(1)
    gather_far(2)
    pair_first(0)
    multiply(1)
    forward(0)
    gather_far(3)
    multiply(2)
    pair_first(1)
    forward(1)
    multiply(3)
    pair_last(0)
    pair_first(2)
    forward(2)
    element(0)
    pair_last(1)
    pair_first(3)
    forward(3)
    pair_share(0)
    element(1)
    pair_last(2)
    line_share(0)
    pair_share(1)
    element(2)
    pair_last(3)
    far_share(0)
    line_share(1)
    pair_share(2)
    element(3)
    back(0)
    far_share(1)
    line_share(2)
    pair_share(3)
    core_sum(0)
    back(1)
    far_share(2)
    line_share(3)
    core_sum(1)
    back(2)
    far_share(3)
    core_sum(2)
    back(3)
    grad_down()
    core_sum(3)
    grad_gate()
    y_sum()
    grad_up()
    z_sum()
    for cp in outs:
        cp.wait()
    for cp in sent:
        cp.wait_send()


SENDS = 128


def per_device(tokens, grad_output, gate_weight, up_weight, down_weight, segment_ids):
    d, f = gate_weight.shape
    cut = (3 * f // 256 + 1) * 128
    vm, dma = pltpu.VMEM, pltpu.SemaphoreType.DMA
    whole = pl.BlockSpec(memory_space=pltpu.VMEM)
    hbm = pl.BlockSpec(memory_space=pl.ANY)
    return pl.pallas_call(
        kernel,
        out_shape=(
            jax.ShapeDtypeStruct(tokens.shape, BF),
            jax.ShapeDtypeStruct(gate_weight.shape, BF),
            jax.ShapeDtypeStruct(up_weight.shape, BF),
            jax.ShapeDtypeStruct(down_weight.shape, BF),
        ),
        in_specs=[hbm, hbm, whole, hbm, hbm, hbm],
        out_specs=(whole, hbm, hbm, hbm),
        scratch_shapes=[
            vm((4, 2, 4, 2, G, d), BF),
            vm((G, d), BF),
            vm((d, f), BF),
            vm((d, f), BF),
            vm((f, d), BF),
            vm((4, 2, 4, G, 3 * f), BF),
            vm((4, 2, G, cut), BF),
            vm((4, 2, G, 3 * f - cut), BF),
            vm((4, 2, 2, G, 3 * f), BF),
            vm((4, G, 3 * f), BF),
            vm((4, G, 3 * f), BF),
            vm((4, 4, G, 3 * f), BF),
            vm((4, 2, 4, G, 3 * f), BF),
            vm((4, 2, 4, G, d), BF),
            vm((4, 4, G, d), BF),
            vm((3, 4, G, d), BF),
            vm((3, 4, G, d), BF),
            vm((4, G, d), BF),
            vm((3, G, d), BF),
            vm((G, d), F32),
            vm((d, TOKENS), BF),
            vm((f, TOKENS), BF),
            vm((TOKENS, d), BF),
            vm((d, f), BF),
            vm((d, f), BF),
            vm((f, d), BF),
            dma((SENDS,)),
            dma((8,)),
            dma((4, 2, 4)),
            dma((4, 2)),
            dma((4, 2)),
            dma((4,)),
            dma((4, 2, 4)),
            dma((4, 2)),
            dma((4,)),
            dma((3,)),
            dma((3,)),
        ],
        compiler_params=pltpu.CompilerParams(
            collective_id=0, has_side_effects=True, vmem_limit_bytes=56 << 20
        ),
    )(tokens, grad_output, segment_ids.reshape(1, TOKENS), gate_weight, up_weight, down_weight)


def solution(mesh):
    in_specs = (
        P("col", "row"),
        P("col", "row"),
        P("row", "col"),
        P("row", "col"),
        P("col", "row"),
        P(),
    )
    out_specs = (P("col", "row"), P("row", "col"), P("row", "col"), P("col", "row"))
    return jax.shard_map(
        per_device, mesh=mesh, in_specs=in_specs, out_specs=out_specs, check_vma=False
    )
```

time: 316 us -> 98.7 us (0.31)
  waiting for transfers between devices: 262 us -> 0 us
  Pallas kernels: 0 us -> 90 us
  matrix products: 26 us -> 0 us
  between operations: 13.8 us -> 0.64 us
  other arithmetic: 3.57 us -> 0 us
    all_gather x2 -> x0, waiting for transfers between devices: 102 us -> none  [the longest x1 55.9 us: per_device(): lax.all_gather(tokens, 'col', axis=0, tiled=True)]
    pallas_call x0 -> x1, Pallas kernels: none -> 90 us  [per_device(): pl.pallas_call(kernel, out_shape=(jax.ShapeDtypeStruct(tokens.shape, BF),...]
    psum x1 -> x0, waiting for transfers between devices: 88.5 us -> none  [per_device(): lax.psum(up_part.astype(jnp.bfloat16), 'row').astype(jnp.float32)]
    reduce_scatter x1 -> x0, waiting for transfers between devices: 70.7 us -> none  [per_device(): lax.psum_scatter((first + second).astype(jnp.bfloat16), 'col', scatter_di...]
    dot_general x8 -> x0, matrix products: 26 us -> none  [the longest x1 4.2 us: per_device(): jnp.einsum('tf,td->fd', hidden, weighted, preferred_element_type=jnp.floa...]
    unnamed x16 -> x8, local copies, waits for them, and re-layouts: 9.39 us -> 7.77 us
  transfers between devices with their start and end apart: 4 -> 0, of which waited for: 4 -> 0; matrix products, arithmetic and copies ran while one was open for 9% -> 0% of each run, Pallas kernels for 0% -> 0%
where the time goes in v1:
time: 98.7 us; the launch traced here: 98.4 us
  Pallas kernels  90 us (91%)
  local copies, waits for them, and re-layouts  7.77 us (8%)
    pallas_call x1, Pallas kernels, per_device(): pl.pallas_call(kernel, out_shape=(jax.ShapeDtypeStruct(tokens.shape, BF),...  90 us
    unnamed x8, local copies, waits for them, and re-layouts  7.77 us

profile of v1, /device:TPU:2, one launch (start us, length us, event | category | flops | bytes accessed | tf_op | source)
XLA Modules:
  0.0 98.4 jit_solution(3526584959175875383)
XLA Ops:
  0.6 90.0 %shard_map.93 = (bf16[16,1024]{1,0:T(8,128)(2,1)}, bf16[1024,896]{1,0:T(8,128)(2,1)}, bf16[1024,896]{1,0:T(8,128)(2,1)}, bf16[896,1024]{1,0:T(8,128)(2,1)}) custom-call(bf16[16,1024]{1,0:T(8,128)(2,1)} %tokens.1, bf16[16,1024]{1,0:T(8,128)(2,1)} %grad.1, s32[1,512]{1,0:T(1,128)} %bitcast.1, bf16[1024,896]{1,0:T(8,128)(2,1)} %gate_w.1, ...), custom_call_target="tpu_custom_call" | custom-call | tf_op jit(solution)/shard_map/pallas_call | solution.py:332
  90.7 1.4 %copy.14 = bf16[16,1024]{1,0:T(8,128)(2,1)} copy(bf16[16,1024]{1,0:T(8,128)(2,1)} %get-tuple-element.8) | data formatting | bytes 65536
  92.0 0.0 copy-start.1
  92.0 3.0 %copy.15 = bf16[1024,896]{1,0:T(8,128)(2,1)} copy(bf16[1024,896]{1,0:T(8,128)(2,1)} %get-tuple-element.9) | data formatting | bytes 3670016
  95.0 0.0 copy-done.1
  95.0 0.0 copy-start
  95.0 1.2 %copy.16 = bf16[1024,896]{1,0:T(8,128)(2,1)} copy(bf16[1024,896]{1,0:T(8,128)(2,1)S(1)} %copy-done.1) | data formatting | bytes 3670016
  96.3 0.9 copy-done
  97.2 1.2 %copy.17 = bf16[896,1024]{1,0:T(8,128)(2,1)} copy(bf16[896,1024]{1,0:T(8,128)(2,1)S(1)} %copy-done) | data formatting | bytes 3670016
Async XLA Ops:
  92.0 3.0 %copy-start.1 = (bf16[1024,896]{1,0:T(8,128)(2,1)S(1)}, bf16[1024,896]{1,0:T(8,128)(2,1)}, u32[]{:S(2)}) copy-start(bf16[1024,896]{1,0:T(8,128)(2,1)} %get-tuple-element.10) | copy-start | bytes 5505028
  95.0 2.2 %copy-start = (bf16[896,1024]{1,0:T(8,128)(2,1)S(1)}, bf16[896,1024]{1,0:T(8,128)(2,1)}, u32[]{:S(2)}) copy-start(bf16[896,1024]{1,0:T(8,128)(2,1)} %get-tuple-element.11) | copy-start | bytes 5505028

commit v2 on v1

v2 whole, which is shorter than its diff:
```python
import functools

import jax
import jax.numpy as jnp
from jax import lax
from jax.experimental import pallas as pl
from jax.experimental.pallas import tpu as pltpu
from jax.sharding import PartitionSpec as P

MESH = pl.DeviceIdType.MESH
BF = jnp.bfloat16
F32 = jnp.float32
TOKENS = 512
SEGS = 64
G = 16
ORDER = (0, 1, 3, 2)
X_SHARE, ALL = 12, 21


def nn(a, b):
    return jnp.dot(a, b, preferred_element_type=F32)


def nt(a, b):
    return lax.dot_general(a, b, (((1,), (1,)), ((), ())), preferred_element_type=F32)


def widths(f):
    wx = 3 * f * X_SHARE // ALL
    wz = 3 * f - wx
    return wx, wz, (wx // 256) * 128, ((wz + 128) // 256) * 128


def kernel(
    tokens, grad, ids, gate_w, up_w, down_w,
    o_tok, o_gate, o_up, o_down,
    tw, gst, gw, uw, dw, px, pz, rpx, rmx, rpz, rmz, lx, lz, zs, zr, zbig, hx, hz,
    gt, sib, ysend, yland, zsend, zland, tok_t, hid_t, w_st,
    ssem, loc, a_recv, rx_recv, rz_recv, lx_recv, lz_recv, zr_recv, zb_recv,
    hx_recv, hz_recv, gx_recv, gz_recv, s_recv, y_recv, zh_recv,
):
    d, f = gw.shape
    wx, wz, cx, cz = widths(f)
    r, c = lax.axis_index("row"), lax.axis_index("col")
    x, zl = r % 4, r // 4
    core, zh, y = c % 2, (c // 2) % 4, c // 8
    xp, xm, x2 = (x + 1) % 4, (x + 3) % 4, (x + 2) % 4

    def at(x=x, zl=zl, y=y, zh=zh, core=core):
        return {"row": zl * 4 + x, "col": (y * 4 + zh) * 2 + core}

    dev_xp, dev_xm, dev_z, dev_core = at(x=xp), at(x=xm), at(zl=1 - zl), at(core=1 - core)
    dev_zh = [at(zh=(zh + k) % 4) for k in (1, 2, 3)]
    dev_y = [at(y=(y + k) % 4) for k in (1, 2, 3)]
    partners = [dev_xp, dev_xm, dev_z, dev_core] + dev_zh + dev_y

    barrier = pltpu.get_barrier_semaphore()
    for p in partners:
        pl.semaphore_signal(barrier, inc=1, device_id=p, device_id_type=MESH)

    first = [
        pltpu.make_async_copy(tokens, tw.at[zh, core, y, 0], loc.at[0]),
        pltpu.make_async_copy(grad, gst, loc.at[1]),
    ]
    weights = [
        pltpu.make_async_copy(gate_w, gw, loc.at[2]),
        pltpu.make_async_copy(up_w, uw, loc.at[3]),
        pltpu.make_async_copy(down_w, dw, loc.at[4]),
    ]
    for cp in first + weights:
        cp.start()

    idr = jnp.broadcast_to(ids[...].astype(F32), (G, TOKENS))
    lane = lax.broadcasted_iota(jnp.int32, (G, TOKENS), 1)
    row = lax.broadcasted_iota(jnp.int32, (G, TOKENS), 0)
    mine = jnp.sum(jnp.where(lane == c * G + row, idr, 0.0), axis=1, keepdims=True)
    count = jnp.sum(jnp.where(idr == mine, 1.0, 0.0), axis=1, keepdims=True)
    weight = (TOKENS / SEGS) / count
    for cp in first:
        cp.wait()
    tw[zh, core, y, 1] = (gst[...].astype(F32) * weight).astype(BF)
    pl.semaphore_wait(barrier, len(partners))

    sent = []

    def push(src, dst, recv, dev):
        cp = pltpu.make_async_remote_copy(
            src_ref=src, dst_ref=dst, send_sem=ssem.at[len(sent)], recv_sem=recv,
            device_id=dev, device_id_type=MESH,
        )
        cp.start()
        sent.append(cp)

    def arrived(ref, recv):
        pltpu.make_async_remote_copy(
            src_ref=ref, dst_ref=ref, send_sem=ssem.at[0], recv_sem=recv,
            device_id=dev_core, device_id_type=MESH,
        ).wait_recv()

    def spread(hh, targets):
        piece = tw.at[hh, core, y]
        for dev in targets:
            push(piece, piece, a_recv.at[hh, core, y], dev)

    def gather_own():
        spread(zh, [dev_zh[0], dev_zh[2], dev_zh[1]])
        spread(zh, [dev_y[0], dev_y[2], dev_y[1], dev_core])

    def gather_far(j):
        hh = (zh + ORDER[j]) % 4
        arrived(tw.at[hh, core, y], a_recv.at[hh, core, y])
        spread(hh, [dev_y[0], dev_y[2], dev_y[1], dev_core])

    def gather_line(j):
        hh = (zh + ORDER[j]) % 4
        for k in (1, 3, 2):
            piece = tw.at[hh, core, (y + k) % 4]
            arrived(piece, a_recv.at[hh, core, (y + k) % 4])
            push(piece, piece, a_recv.at[hh, core, (y + k) % 4], dev_core)

    def multiply(j):
        hh = (zh + ORDER[j]) % 4
        for yy in range(4):
            arrived(tw.at[hh, 1 - core, yy], a_recv.at[hh, 1 - core, yy])
        t = tw[hh, :, :, 0].reshape(8 * G, d)
        w = tw[hh, :, :, 1].reshape(8 * G, d)
        if j == 0:
            for cp in weights:
                cp.wait()
        p = nn(t, gw[...]).astype(BF).reshape(2, 4, G, f)
        px[j, :, :, :, 0:f] = p
        p = nn(t, uw[...]).astype(BF).reshape(2, 4, G, f)
        px[j, :, :, :, f:wx] = p[:, :, :, : wx - f]
        relay_x(j)
        pz[j, :, :, :, : 2 * f - wx] = p[:, :, :, wx - f :]
        pz[j, :, :, :, 2 * f - wx :] = nt(w, dw[...]).astype(BF).reshape(2, 4, G, f)
        push(pz.at[j, 1 - zl], zbig.at[j], zb_recv.at[j], dev_z)
        tok_t[:, j * 8 * G : (j + 1) * 8 * G] = t.T
        w_st[j * 8 * G : (j + 1) * 8 * G, :] = w

    def relay_x(j):
        push(px.at[j, :, x2, :, :cx], rpx.at[j], rx_recv.at[j, 0], dev_xp)
        push(px.at[j, :, x2, :, cx:], rmx.at[j], rx_recv.at[j, 1], dev_xm)
        push(px.at[j, :, xp, :, cx:], lx.at[j, 0, :, :, cx:], lx_recv.at[j, 0, 1], dev_xp)
        push(px.at[j, :, xm, :, :cx], lx.at[j, 1, :, :, :cx], lx_recv.at[j, 1, 0], dev_xm)

    def relay_z(j):
        push(pz.at[j, zl, x2, :, :cz], rpz.at[j], rz_recv.at[j, 0], dev_xp)
        push(pz.at[j, zl, x2, :, cz:], rmz.at[j], rz_recv.at[j, 1], dev_xm)
        push(pz.at[j, zl, xp, :, cz:], lz.at[j, 0, :, cz:], lz_recv.at[j, 0, 1], dev_xp)
        push(pz.at[j, zl, xm, :, :cz], lz.at[j, 1, :, :cz], lz_recv.at[j, 1, 0], dev_xm)

    def pair_first(j):
        arrived(zbig.at[j], zb_recv.at[j])
        pz[j, zl] = (pz[j, zl].astype(F32) + zbig[j].astype(F32)).astype(BF)
        relay_z(j)

    def forward_x(j):
        arrived(rpx.at[j], rx_recv.at[j, 0])
        rpx[j] = (px[j, :, xp, :, :cx].astype(F32) + rpx[j].astype(F32)).astype(BF)
        push(rpx.at[j], lx.at[j, 0, :, :, :cx], lx_recv.at[j, 0, 0], dev_xp)
        arrived(rmx.at[j], rx_recv.at[j, 1])
        rmx[j] = (px[j, :, xm, :, cx:].astype(F32) + rmx[j].astype(F32)).astype(BF)
        push(rmx.at[j], lx.at[j, 1, :, :, cx:], lx_recv.at[j, 1, 1], dev_xm)

    def forward_z(j):
        arrived(rpz.at[j], rz_recv.at[j, 0])
        rpz[j] = (pz[j, zl, xp, :, :cz].astype(F32) + rpz[j].astype(F32)).astype(BF)
        push(rpz.at[j], lz.at[j, 0, :, :cz], lz_recv.at[j, 0, 0], dev_xp)
        arrived(rmz.at[j], rz_recv.at[j, 1])
        rmz[j] = (pz[j, zl, xm, :, cz:].astype(F32) + rmz[j].astype(F32)).astype(BF)
        push(rmz.at[j], lz.at[j, 1, :, cz:], lz_recv.at[j, 1, 1], dev_xm)

    def sum_x(j, z):
        return px[j, z, x].astype(F32) + lx[j, 0, z].astype(F32) + lx[j, 1, z].astype(F32)

    def pair_last(j):
        for n in range(2):
            arrived(lx.at[j, n, :, :, :cx], lx_recv.at[j, n, 0])
            arrived(lx.at[j, n, :, :, cx:], lx_recv.at[j, n, 1])
        zs[j] = sum_x(j, 1 - zl).astype(BF)
        push(zs.at[j], zr.at[j], zr_recv.at[j], dev_z)

    def share_x(j, z, xx, targets):
        piece = hx.at[j, z, xx]
        for dev in targets:
            push(piece, piece, hx_recv.at[j, z, xx], dev)

    def share_z(j, xx, targets):
        piece = hz.at[j, zl, xx]
        for dev in targets:
            push(piece, piece, hz_recv.at[j, zl, xx], dev)

    def element(j):
        for n in range(2):
            arrived(lz.at[j, n, :, :cz], lz_recv.at[j, n, 0])
            arrived(lz.at[j, n, :, cz:], lz_recv.at[j, n, 1])
        arrived(zr.at[j], zr_recv.at[j])
        tx = sum_x(j, zl) + zr[j].astype(F32)
        tz = pz[j, zl, x].astype(F32) + lz[j, 0].astype(F32) + lz[j, 1].astype(F32)
        gate, dh = tx[:, :f], tz[:, 2 * f - wx :]
        up = jnp.concatenate([tx[:, f:], tz[:, : 2 * f - wx]], axis=1)
        sig = jax.nn.sigmoid(gate)
        act = gate * sig
        hx[j, zl, x, :, 0:f] = (act * up).astype(BF)
        d_gate = (dh * up * sig * (1.0 + gate * (1.0 - sig))).astype(BF)
        hx[j, zl, x, :, f:wx] = d_gate[:, : wx - f]
        hz[j, zl, x, :, : 2 * f - wx] = d_gate[:, wx - f :]
        hz[j, zl, x, :, 2 * f - wx :] = (dh * act).astype(BF)
        share_x(j, zl, x, [dev_z, dev_xp, dev_xm])
        share_z(j, x, [dev_xp, dev_xm, dev_z])

    def pair_share(j):
        arrived(hx.at[j, 1 - zl, x], hx_recv.at[j, 1 - zl, x])
        share_x(j, 1 - zl, x, [dev_xp, dev_xm])

    def line_share_x(j):
        for src, half, dev, n in ((xm, slice(0, cx), dev_xp, 0), (xp, slice(cx, wx), dev_xm, 1)):
            for z in range(2):
                arrived(hx.at[j, z, src], hx_recv.at[j, z, src])
            piece = hx.at[j, :, src, :, half]
            push(piece, piece, gx_recv.at[j, n], dev)

    def line_share_z(j):
        for src, half, dev, n in ((xm, slice(0, cz), dev_xp, 0), (xp, slice(cz, wz), dev_xm, 1)):
            arrived(hz.at[j, zl, src], hz_recv.at[j, zl, src])
            piece = hz.at[j, zl, src, :, half]
            push(piece, piece, gz_recv.at[j, n], dev)
            share_z(j, src, [dev_z])

    def far_share(j):
        arrived(hz.at[j, zl, x2, :, :cz], gz_recv.at[j, 0])
        arrived(hz.at[j, zl, x2, :, cz:], gz_recv.at[j, 1])
        share_z(j, x2, [dev_z])

    def d_gate_of(j):
        left = hx[j, :, :, :, f:wx]
        right = hz[j, :, :, :, : 2 * f - wx]
        return jnp.concatenate([left, right], axis=-1).reshape(8 * G, f)

    def d_up_of(j):
        return hz[j, :, :, :, 2 * f - wx :].reshape(8 * G, f)

    def back(j):
        arrived(hx.at[j, :, x2, :, :cx], gx_recv.at[j, 0])
        arrived(hx.at[j, :, x2, :, cx:], gx_recv.at[j, 1])
        for xx in range(4):
            arrived(hz.at[j, 1 - zl, xx], hz_recv.at[j, 1 - zl, xx])
        back_sum = nt(d_gate_of(j), gw[...]) + nt(d_up_of(j), uw[...])
        gt[j] = back_sum.astype(BF).reshape(2, 4, G, d)
        push(gt.at[j, 1 - core], sib.at[j], s_recv.at[j], dev_core)
        hid_t[:, j * 8 * G : (j + 1) * 8 * G] = hx[j, :, :, :, 0:f].reshape(8 * G, f).T

    def core_sum(j):
        arrived(sib.at[j], s_recv.at[j])
        ysend[j] = (gt[j, core].astype(F32) + sib[j].astype(F32)).astype(BF)
        for k in (1, 0, 2):
            push(ysend.at[j, (y + k + 1) % 4], yland.at[j, k], y_recv.at[j, k], dev_y[k])

    def y_total(j):
        total = gt[j, core, y].astype(F32) + sib[j, y].astype(F32)
        for k in range(3):
            arrived(yland.at[j, k], y_recv.at[j, k])
            total = total + yland[j, k].astype(F32)
        return total

    def y_sum(j):
        zsend[j - 1] = y_total(j).astype(BF)
        push(zsend.at[j - 1], zland.at[j - 1], zh_recv.at[j - 1], dev_zh[ORDER[j] - 1])

    def finish():
        total = y_total(0)
        for k in range(3):
            arrived(zland.at[k], zh_recv.at[k])
            total = total + zland[k].astype(F32)
        o_tok[...] = total.astype(BF)

    def weight_grad(lhs, rhs, out):
        rows = 256 if lhs.shape[0] % 256 == 0 else 128
        for m in range(0, lhs.shape[0], rows):
            out[m : m + rows, :] = nn(lhs[m : m + rows, :], rhs).astype(BF)

    def grad_down():
        weight_grad(hid_t, w_st[...], o_down)

    def grad_gate():
        weight_grad(tok_t, jnp.concatenate([d_gate_of(j) for j in range(4)], axis=0), o_gate)

    def grad_up():
        weight_grad(tok_t, jnp.concatenate([d_up_of(j) for j in range(4)], axis=0), o_up)

    gather_own()
    gather_far(2)
    gather_line(0)
    gather_far(1)
    multiply(0)
    gather_line(2)
    gather_far(3)
    forward_x(0)
    gather_line(1)
    multiply(2)
    pair_first(0)
    gather_line(3)
    multiply(1)
    forward_x(2)
    multiply(3)
    pair_first(2)
    forward_x(1)
    pair_last(2)
    pair_first(1)
    forward_z(2)
    forward_x(3)
    pair_last(0)
    forward_z(0)
    pair_last(1)
    forward_z(1)
    pair_first(3)
    element(2)
    pair_last(3)
    forward_z(3)
    element(1)
    pair_share(2)
    line_share_z(2)
    element(3)
    line_share_z(1)
    pair_share(1)
    line_share_x(2)
    far_share(2)
    far_share(1)
    pair_share(3)
    line_share_z(3)
    line_share_x(1)
    element(0)
    back(2)
    far_share(3)
    line_share_x(3)
    back(1)
    pair_share(0)
    line_share_z(0)
    core_sum(2)
    back(3)
    line_share_x(0)
    far_share(0)
    core_sum(1)
    core_sum(3)
    y_sum(2)
    back(0)
    y_sum(1)
    grad_down()
    y_sum(3)
    core_sum(0)
    grad_gate()
    grad_up()
    finish()
    for cp in sent:
        cp.wait_send()


SENDS = 192
VMEM_LIMIT = 58 << 20


def per_device(tokens, grad_output, gate_weight, up_weight, down_weight, segment_ids):
    d, f = gate_weight.shape
    wx, wz, cx, cz = widths(f)
    vm, dma = pltpu.VMEM, pltpu.SemaphoreType.DMA
    whole = pl.BlockSpec(memory_space=pltpu.VMEM)
    hbm = pl.BlockSpec(memory_space=pl.ANY)
    return pl.pallas_call(
        kernel,
        out_shape=(
            vm(tokens.shape, BF),
            vm(gate_weight.shape, BF),
            vm(up_weight.shape, BF),
            vm(down_weight.shape, BF),
        ),
        in_specs=[hbm, hbm, whole, hbm, hbm, hbm],
        out_specs=(whole, whole, whole, whole),
        scratch_shapes=[
            vm((4, 2, 4, 2, G, d), BF),
            vm((G, d), BF),
            vm((d, f), BF),
            vm((d, f), BF),
            vm((f, d), BF),
            vm((4, 2, 4, G, wx), BF),
            vm((4, 2, 4, G, wz), BF),
            vm((4, 2, G, cx), BF),
            vm((4, 2, G, wx - cx), BF),
            vm((4, G, cz), BF),
            vm((4, G, wz - cz), BF),
            vm((4, 2, 2, G, wx), BF),
            vm((4, 2, G, wz), BF),
            vm((4, G, wx), BF),
            vm((4, G, wx), BF),
            vm((4, 4, G, wz), BF),
            vm((4, 2, 4, G, wx), BF),
            vm((4, 2, 4, G, wz), BF),
            vm((4, 2, 4, G, d), BF),
            vm((4, 4, G, d), BF),
            vm((4, 4, G, d), BF),
            vm((4, 3, G, d), BF),
            vm((3, G, d), BF),
            vm((3, G, d), BF),
            vm((d, TOKENS), BF),
            vm((f, TOKENS), BF),
            vm((TOKENS, d), BF),
            dma((SENDS,)),
            dma((5,)),
            dma((4, 2, 4)),
            dma((4, 2)),
            dma((4, 2)),
            dma((4, 2, 2)),
            dma((4, 2, 2)),
            dma((4,)),
            dma((4,)),
            dma((4, 2, 4)),
            dma((4, 2, 4)),
            dma((4, 2)),
            dma((4, 2)),
            dma((4,)),
            dma((4, 3)),
            dma((3,)),
        ],
        compiler_params=pltpu.CompilerParams(
            collective_id=0, has_side_effects=True, vmem_limit_bytes=VMEM_LIMIT
        ),
    )(tokens, grad_output, segment_ids.reshape(1, TOKENS), gate_weight, up_weight, down_weight)


def solution(mesh):
    in_specs = (
        P("col", "row"),
        P("col", "row"),
        P("row", "col"),
        P("row", "col"),
        P("col", "row"),
        P(),
    )
    out_specs = (P("col", "row"), P("row", "col"), P("row", "col"), P("col", "row"))
    return jax.shard_map(
        per_device, mesh=mesh, in_specs=in_specs, out_specs=out_specs, check_vma=False
    )
```

time: 98.7 us -> 78.7 us (0.80)
  Pallas kernels: 90 us -> 73.7 us
  local copies, waits for them, and re-layouts: 7.77 us -> 4.3 us
    pallas_call x1, Pallas kernels: 90 us -> 73.7 us  [per_device(): pl.pallas_call(kernel, out_shape=(vm(tokens.shape, BF), vm(gate_weight.sh...]
    unnamed x8 -> x4, local copies, waits for them, and re-layouts: 7.77 us -> 4.3 us
where the time goes in v2:
time: 78.7 us; the launch traced here: 78.6 us
  Pallas kernels  73.7 us (94%)
  local copies, waits for them, and re-layouts  4.3 us (5%)
    pallas_call x1, Pallas kernels, per_device(): pl.pallas_call(kernel, out_shape=(vm(tokens.shape, BF), vm(gate_weight.sh...  73.7 us
    unnamed x4, local copies, waits for them, and re-layouts  4.3 us

profile of v2, /device:TPU:2, one launch (start us, length us, event | category | flops | bytes accessed | tf_op | source)
XLA Modules:
  0.0 78.6 jit_solution(5523762709648614127)
XLA Ops:
  0.6 73.7 %shard_map.93 = (bf16[16,1024]{1,0:T(8,128)(2,1)S(1)}, bf16[1024,896]{1,0:T(8,128)(2,1)S(1)}, bf16[1024,896]{1,0:T(8,128)(2,1)S(1)}, bf16[896,1024]{1,0:T(8,128)(2,1)S(1)}) custom-call(bf16[16,1024]{1,0:T(8,128)(2,1)} %tokens.1, bf16[16,1024]{1,0:T(8,128)(2,1)} %grad.1, s32[1,512]{1,0:T(1,128)} %bitcast.1, bf16[1024,896]{1,0:T(8,128)(2,1)} %gate_w.1, ...), custom_call_target="tpu_custom_call" | custom-call | tf_op jit(solution)/shard_map/pallas_call | solution.py:369
  74.3 0.6 copy.14
  74.9 1.2 %copy.15 = bf16[1024,896]{1,0:T(8,128)(2,1)} copy(bf16[1024,896]{1,0:T(8,128)(2,1)S(1)} %get-tuple-element.5) | data formatting | bytes 3670016
  76.2 1.2 %copy.16 = bf16[1024,896]{1,0:T(8,128)(2,1)} copy(bf16[1024,896]{1,0:T(8,128)(2,1)S(1)} %get-tuple-element.6) | data formatting | bytes 3670016
  77.4 1.2 %copy.17 = bf16[896,1024]{1,0:T(8,128)(2,1)} copy(bf16[896,1024]{1,0:T(8,128)(2,1)S(1)} %get-tuple-element.7) | data formatting | bytes 3670016

commit v3 on v2

--- a/solution.py
+++ b/solution.py
@@ -34,10 +34,10 @@
 def kernel(
     tokens, grad, ids, gate_w, up_w, down_w,
     o_tok, o_gate, o_up, o_down,
-    tw, gst, gw, uw, dw, px, pz, rpx, rmx, rpz, rmz, lx, lz, zs, zr, zbig, hx, hz,
-    gt, sib, ysend, yland, zsend, zland, tok_t, hid_t, w_st,
+    tw, gst, idv, gw, uw, dw, px, pz, rpx, rmx, rpz, rmz, lx, lz, zs, zr, zbig, hx, hz,
+    gt, sib, ysend, yland, ycross, zsend, zland, tok_t, hid_t, w_st,
     ssem, loc, a_recv, rx_recv, rz_recv, lx_recv, lz_recv, zr_recv, zb_recv,
-    hx_recv, hz_recv, gx_recv, gz_recv, s_recv, y_recv, zh_recv,
+    hx_recv, hz_recv, gx_recv, gz_recv, s_recv, y_recv, yc_recv, zh_recv,
 ):
     d, f = gw.shape
     wx, wz, cx, cz = widths(f)
@@ -52,7 +52,8 @@
     dev_xp, dev_xm, dev_z, dev_core = at(x=xp), at(x=xm), at(zl=1 - zl), at(core=1 - core)
     dev_zh = [at(zh=(zh + k) % 4) for k in (1, 2, 3)]
     dev_y = [at(y=(y + k) % 4) for k in (1, 2, 3)]
-    partners = [dev_xp, dev_xm, dev_z, dev_core] + dev_zh + dev_y
+    dev_yc = [at(y=(y + k) % 4, core=1 - core) for k in (1, 2, 3)]
+    partners = [dev_xp, dev_xm, dev_z, dev_core] + dev_zh + dev_y + dev_yc
 
     barrier = pltpu.get_barrier_semaphore()
     for p in partners:
@@ -61,6 +62,7 @@
     first = [
         pltpu.make_async_copy(tokens, tw.at[zh, core, y, 0], loc.at[0]),
         pltpu.make_async_copy(grad, gst, loc.at[1]),
+        pltpu.make_async_copy(ids, idv, loc.at[5]),
     ]
     weights = [
         pltpu.make_async_copy(gate_w, gw, loc.at[2]),
@@ -70,14 +72,14 @@
     for cp in first + weights:
         cp.start()
 
-    idr = jnp.broadcast_to(ids[...].astype(F32), (G, TOKENS))
+    for cp in first:
+        cp.wait()
+    idr = jnp.broadcast_to(idv[...].astype(F32), (G, TOKENS))
     lane = lax.broadcasted_iota(jnp.int32, (G, TOKENS), 1)
     row = lax.broadcasted_iota(jnp.int32, (G, TOKENS), 0)
     mine = jnp.sum(jnp.where(lane == c * G + row, idr, 0.0), axis=1, keepdims=True)
     count = jnp.sum(jnp.where(idr == mine, 1.0, 0.0), axis=1, keepdims=True)
     weight = (TOKENS / SEGS) / count
-    for cp in first:
-        cp.wait()
     tw[zh, core, y, 1] = (gst[...].astype(F32) * weight).astype(BF)
     pl.semaphore_wait(barrier, len(partners))
 
@@ -248,7 +250,14 @@
             arrived(hz.at[j, 1 - zl, xx], hz_recv.at[j, 1 - zl, xx])
         back_sum = nt(d_gate_of(j), gw[...]) + nt(d_up_of(j), uw[...])
         gt[j] = back_sum.astype(BF).reshape(2, 4, G, d)
-        push(gt.at[j, 1 - core], sib.at[j], s_recv.at[j], dev_core)
+        if j > 0:
+            push(gt.at[j, 1 - core], sib.at[j], s_recv.at[j], dev_core)
+        else:
+            for k in (1, 0, 2):
+                yy = (y + k + 1) % 4
+                push(gt.at[j, core, yy], yland.at[j, k], y_recv.at[j, k], dev_y[k])
+                push(gt.at[j, 1 - core, yy], ycross.at[k], yc_recv.at[k], dev_yc[k])
+            push(gt.at[j, 1 - core, y], sib.at[j, y], s_recv.at[j], dev_core)
         hid_t[:, j * 8 * G : (j + 1) * 8 * G] = hx[j, :, :, :, 0:f].reshape(8 * G, f).T
 
     def core_sum(j):
@@ -269,7 +278,11 @@
         push(zsend.at[j - 1], zland.at[j - 1], zh_recv.at[j - 1], dev_zh[ORDER[j] - 1])
 
     def finish():
+        arrived(sib.at[0, y], s_recv.at[0])
         total = y_total(0)
+        for k in range(3):
+            arrived(ycross.at[k], yc_recv.at[k])
+            total = total + ycross[k].astype(F32)
         for k in range(3):
             arrived(zland.at[k], zh_recv.at[k])
             total = total + zland[k].astype(F32)
@@ -348,7 +361,6 @@
     y_sum(1)
     grad_down()
     y_sum(3)
-    core_sum(0)
     grad_gate()
     grad_up()
     finish()
@@ -358,6 +370,15 @@
 
 SENDS = 192
 VMEM_LIMIT = 58 << 20
+
+
+def store(a, b, c, d, a_out, b_out, c_out, d_out, sems):
+    pairs = ((a, a_out), (b, b_out), (c, c_out), (d, d_out))
+    copies = [pltpu.make_async_copy(src, dst, sems.at[n]) for n, (src, dst) in enumerate(pairs)]
+    for cp in copies:
+        cp.start()
+    for cp in copies:
+        cp.wait()
 
 
 def per_device(tokens, grad_output, gate_weight, up_weight, down_weight, segment_ids):
@@ -366,7 +387,7 @@
     vm, dma = pltpu.VMEM, pltpu.SemaphoreType.DMA
     whole = pl.BlockSpec(memory_space=pltpu.VMEM)
     hbm = pl.BlockSpec(memory_space=pl.ANY)
-    return pl.pallas_call(
+    held = pl.pallas_call(
         kernel,
         out_shape=(
             vm(tokens.shape, BF),
@@ -374,11 +395,12 @@
             vm(up_weight.shape, BF),
             vm(down_weight.shape, BF),
         ),
-        in_specs=[hbm, hbm, whole, hbm, hbm, hbm],
+        in_specs=[hbm] * 6,
         out_specs=(whole, whole, whole, whole),
         scratch_shapes=[
             vm((4, 2, 4, 2, G, d), BF),
             vm((G, d), BF),
+            vm((1, TOKENS), jnp.int32),
             vm((d, f), BF),
             vm((d, f), BF),
             vm((f, d), BF),
@@ -401,11 +423,12 @@
             vm((4, 3, G, d), BF),
             vm((3, G, d), BF),
             vm((3, G, d), BF),
+            vm((3, G, d), BF),
             vm((d, TOKENS), BF),
             vm((f, TOKENS), BF),
             vm((TOKENS, d), BF),
             dma((SENDS,)),
-            dma((5,)),
+            dma((6,)),
             dma((4, 2, 4)),
             dma((4, 2)),
             dma((4, 2)),
@@ -420,11 +443,20 @@
             dma((4,)),
             dma((4, 3)),
             dma((3,)),
+            dma((3,)),
         ],
         compiler_params=pltpu.CompilerParams(
             collective_id=0, has_side_effects=True, vmem_limit_bytes=VMEM_LIMIT
         ),
     )(tokens, grad_output, segment_ids.reshape(1, TOKENS), gate_weight, up_weight, down_weight)
+    return pl.pallas_call(
+        store,
+        out_shape=tuple(jax.ShapeDtypeStruct(a.shape, a.dtype) for a in held),
+        in_specs=[hbm] * 4,
+        out_specs=(hbm,) * 4,
+        scratch_shapes=[dma((4,))],
+        compiler_params=pltpu.CompilerParams(vmem_limit_bytes=1 << 20),
+    )(*[pltpu.with_memory_space_constraint(a, pltpu.VMEM) for a in held])
 
 
 def solution(mesh):

time: 78.7 us -> 76.7 us (0.975)
  local copies, waits for them, and re-layouts: 4.3 us -> 0 us
  Pallas kernels: 73.7 us -> 75.9 us
    unnamed x4 -> x0, local copies, waits for them, and re-layouts: 4.3 us -> none
    pallas_call x0 -> x1, Pallas kernels: none -> 2.48 us  [per_device(): pl.pallas_call(store, out_shape=tuple((jax.ShapeDtypeStruct(a.shape, a.dt...]
where the time goes in v3:
time: 76.7 us; the launch traced here: 76.6 us
  Pallas kernels  75.9 us (99%)
    pallas_call x1, Pallas kernels, per_device(): pl.pallas_call(kernel, out_shape=(vm(tokens.shape, BF), vm(gate_weight.sh...  73.5 us
    pallas_call x1, Pallas kernels, per_device(): pl.pallas_call(store, out_shape=tuple((jax.ShapeDtypeStruct(a.shape, a.dt...  2.48 us

profile of v3, /device:TPU:2, one launch (start us, length us, event | category | flops | bytes accessed | tf_op | source)
XLA Modules:
  0.0 76.6 jit_solution(3128397414218178498)
XLA Ops:
  0.6 73.5 %shard_map.93 = (bf16[16,1024]{1,0:T(8,128)(2,1)S(1)}, bf16[1024,896]{1,0:T(8,128)(2,1)S(1)}, bf16[1024,896]{1,0:T(8,128)(2,1)S(1)}, bf16[896,1024]{1,0:T(8,128)(2,1)S(1)}) custom-call(bf16[16,1024]{1,0:T(8,128)(2,1)} %tokens.1, bf16[16,1024]{1,0:T(8,128)(2,1)} %grad.1, s32[1,512]{1,0:T(1,128)} %bitcast.1, bf16[1024,896]{1,0:T(8,128)(2,1)} %gate_w.1, ...), custom_call_target="tpu_custom_call" | custom-call | tf_op jit(solution)/shard_map/pallas_call | solution.py:390
  74.1 2.5 %shard_map.94 = (bf16[16,1024]{1,0:T(8,128)(2,1)}, bf16[1024,896]{1,0:T(8,128)(2,1)}, bf16[1024,896]{1,0:T(8,128)(2,1)}, bf16[896,1024]{1,0:T(8,128)(2,1)}) custom-call(bf16[16,1024]{1,0:T(8,128)(2,1)S(1)} %get-tuple-element.8.a, bf16[1024,896]{1,0:T(8,128)(2,1)S(1)} %get-tuple-element.9.b, bf16[1024,896]{1,0:T(8,128)(2,1)S(1)} %get-tuple-element.10.c, ...), custom_call_target="tpu_custom_call" | custom-call | tf_op jit(solution)/shard_map/pallas_call | solution.py:452

commit v4 on v3

--- a/solution.py
+++ b/solution.py
@@ -129,14 +129,13 @@
         if j == 0:
             for cp in weights:
                 cp.wait()
-        p = nn(t, gw[...]).astype(BF).reshape(2, 4, G, f)
-        px[j, :, :, :, 0:f] = p
         p = nn(t, uw[...]).astype(BF).reshape(2, 4, G, f)
         px[j, :, :, :, f:wx] = p[:, :, :, : wx - f]
-        relay_x(j)
         pz[j, :, :, :, : 2 * f - wx] = p[:, :, :, wx - f :]
         pz[j, :, :, :, 2 * f - wx :] = nt(w, dw[...]).astype(BF).reshape(2, 4, G, f)
         push(pz.at[j, 1 - zl], zbig.at[j], zb_recv.at[j], dev_z)
+        px[j, :, :, :, 0:f] = nn(t, gw[...]).astype(BF).reshape(2, 4, G, f)
+        relay_x(j)
         tok_t[:, j * 8 * G : (j + 1) * 8 * G] = t.T
         w_st[j * 8 * G : (j + 1) * 8 * G, :] = w
 

time: 76.7 us -> 77.2 us (level)
  no operation moved by 1% of the time
where the time goes in v4:
time: 77.2 us; the launch traced here: 77 us
  Pallas kernels  76.3 us (99%)
    pallas_call x1, Pallas kernels, per_device(): pl.pallas_call(kernel, out_shape=(vm(tokens.shape, BF), vm(gate_weight.sh...  73.8 us
    pallas_call x1, Pallas kernels, per_device(): pl.pallas_call(store, out_shape=tuple((jax.ShapeDtypeStruct(a.shape, a.dt...  2.48 us

profile of v4, /device:TPU:2, one launch (start us, length us, event | category | flops | bytes accessed | tf_op | source)
XLA Modules:
  0.0 77.0 jit_solution(15442260326565988204)
XLA Ops:
  0.6 73.8 %shard_map.93 = (bf16[16,1024]{1,0:T(8,128)(2,1)S(1)}, bf16[1024,896]{1,0:T(8,128)(2,1)S(1)}, bf16[1024,896]{1,0:T(8,128)(2,1)S(1)}, bf16[896,1024]{1,0:T(8,128)(2,1)S(1)}) custom-call(bf16[16,1024]{1,0:T(8,128)(2,1)} %tokens.1, bf16[16,1024]{1,0:T(8,128)(2,1)} %grad.1, s32[1,512]{1,0:T(1,128)} %bitcast.1, bf16[1024,896]{1,0:T(8,128)(2,1)} %gate_w.1, ...), custom_call_target="tpu_custom_call" | custom-call | tf_op jit(solution)/shard_map/pallas_call | solution.py:389
  74.5 2.5 %shard_map.94 = (bf16[16,1024]{1,0:T(8,128)(2,1)}, bf16[1024,896]{1,0:T(8,128)(2,1)}, bf16[1024,896]{1,0:T(8,128)(2,1)}, bf16[896,1024]{1,0:T(8,128)(2,1)}) custom-call(bf16[16,1024]{1,0:T(8,128)(2,1)S(1)} %get-tuple-element.8.a, bf16[1024,896]{1,0:T(8,128)(2,1)S(1)} %get-tuple-element.9.b, bf16[1024,896]{1,0:T(8,128)(2,1)S(1)} %get-tuple-element.10.c, ...), custom_call_target="tpu_custom_call" | custom-call | tf_op jit(solution)/shard_map/pallas_call | solution.py:451
